TPU v7x, 256 devices: a whole 4x4x8 slice. The times are simulated.
256 devices in a mesh: band: 16 (over z, core), gvec: 16 (over y, x).
Axes of the slice: x: 4, y: 4, z: 8, core: 2. Of those that a mesh axis runs over, the one named last changes fastest.
Arguments:
- pair_density: bfloat16 [768, 16, 60000], P('band', None, 'gvec'), may hold values from -6 to 6
- eigvecs: bfloat16 [60000, 2000], P('gvec', 'band'), may hold values from -0.0234375 to 0.0234375
- subspace: bfloat16 [4, 2000, 2000], P(None, 'gvec'), may hold values from -0.125 to 0.125
- counts: int32 [16], P('band'), may hold values from 1 to 48, as said below
- freq_index: int32 [768, 16], P('band'), may hold values from 0 to 3
- band_weight: float32 [768], P('band'), may hold values from 0.3 to 3
Outputs:
- coef: float32 [768, 16, 2000], P('band', None, 'gvec')
- sigma: float32 [16], replicated
Inputs may be any that keep to these rules, and one draw needn't show every extreme that they name: `counts`: each group has at least one live slot; some group has all 48 slots live.
All inputs are finite; a program needn't handle non-finite values.
Results may differ from a plain program's by a relative error of at most 0.0026.
Values may be sent and summed in bfloat16 or wider, within the bound.
No kernel may reach another device: no remote copies, remote signals or barrier semaphores. Data moves between devices by JAX's collectives and lax.ppermute only.
A program may use at most 128 MiB of HBM per device.

v0:
```python
import math

import jax
import jax.numpy as jnp
from jax import lax
from jax.sharding import PartitionSpec as P

NEIG = 2000


def local(pair_density, eigvecs, subspace, counts, freq_index, band_weight):
    slots, states, gcount = pair_density.shape
    nrows = slots * states
    share = subspace.shape[1]
    flat_rows = pair_density.reshape(nrows, gcount)
    live = (jnp.arange(slots, dtype=jnp.int32) < counts[0]).astype(jnp.float32)
    live_rows = jnp.repeat(live, states)[:, None]
    partial_sum = (
        jnp.dot(
            flat_rows,
            lax.all_gather(eigvecs, "band", axis=1, tiled=True),
            preferred_element_type=jnp.float32,
        )
        * live_rows
    )
    offset = lax.axis_index("gvec") * share
    summed = lax.psum(partial_sum, "gvec")
    own_coef = lax.dynamic_slice_in_dim(summed, offset, share, 1)
    rounded = summed.astype(jnp.bfloat16)
    mine = lax.dynamic_slice_in_dim(rounded, offset, share, 1).astype(jnp.float32)
    applied = jnp.einsum("rs,wts->wrt", rounded, subspace, preferred_element_type=jnp.float32)
    quad = jnp.sum(mine[None, :, :] * applied, axis=2)
    nodes = jnp.arange(quad.shape[0], dtype=jnp.int32)
    chosen = freq_index.reshape(-1)[None, :] == nodes[:, None]
    picked = jnp.sum(jnp.where(chosen, quad, jnp.float32(0.0)), axis=0)
    weights = (band_weight * live)[:, None]
    terms = jnp.sum(picked.reshape(slots, states) * weights, axis=0)
    total = lax.psum(terms, ("band", "gvec"))
    scale_factor = math.sqrt(NEIG * lax.axis_size("band") * slots)
    sigma = -total / jnp.float32(scale_factor)
    coef = own_coef.reshape(slots, states, share)
    return (coef, sigma)


def solution(mesh):
    in_specs = (
        P("band", None, "gvec"),
        P("gvec", "band"),
        P(None, "gvec", None),
        P("band"),
        P("band", None),
        P("band"),
    )
    out_specs = (P("band", None, "gvec"), P())
    return jax.shard_map(local, mesh=mesh, in_specs=in_specs, out_specs=out_specs, check_vma=False)
```

profile of v0, /device:TPU:1, one launch (start us, length us, event | category | flops | bytes accessed | tf_op | source)
XLA Modules:
  0.0 396.1 jit_solution(16182712566362063675)
XLA Ops:
  7.2 0.0 copy-start
  7.2 0.0 all-gather.3.cloned.1.call-start
  7.2 0.7 all-gather.3.cloned.1.call-update
  7.9 0.0 all-reduce.2.cloned.1.call-start
  8.6 0.1 broadcast_in_dim.10
  8.7 0.1 mul.33
  8.8 94.1 %all-gather.3.cloned.1.call-done = bf16[16,125,3750]{1,2,0:T(8,128)(2,1)} async-done(((bf16[1,125,3750]{1,2,0:T(8,128)(2,1)}), bf16[16,125,3750]{1,2,0:T(8,128)(2,1)}) %all-gather.3.cloned.1.call-update) | async-done | bytes 15000016 | tf_op jit(solution)/shard_map/all_gather | solution.py:21
  102.9 24.0 %copy.17 = bf16[16,125,3750]{1,0,2:T(8,128)(2,1)} copy(bf16[16,125,3750]{1,2,0:T(8,128)(2,1)} %all-gather.3.cloned.1.call-done) | data formatting | bytes 30000000 | tf_op jit(solution)/shard_map/all_gather | solution.py:21
  126.9 28.3 %reshape.21 = bf16[2000,3750]{0,1:T(8,128)(2,1)} reshape(bf16[16,125,3750]{1,0,2:T(8,128)(2,1)} %copy.17) | data formatting | bytes 30000000
  155.1 19.6 %convolution_multiply_fusion = f32[768,2000]{0,1:T(8,128)} fusion(bf16[768,3750]{1,0:T(8,128)(2,1)} %bitcast.23, bf16[2000,3750]{0,1:T(8,128)(2,1)} %reshape.21, f32[768]{0:T(1024)S(1)} %mul.33), kind=kOutput, calls=%fused_computation | convolution fusion | flops 11521536000 | bytes 26907072 | tf_op jit(solution)/shard_map/dot_general | solution.py:19
  174.7 0.0 copy-start.1
  174.7 0.0 copy-start.2
  174.7 0.0 all-reduce.2.cloned.1.call-update
  174.8 0.7 copy-done.1
  175.4 0.1 copy.19
  175.5 0.1 eq.15
  175.6 0.0 copy-done.2
  175.6 128.5 %all-reduce.2.cloned.1.call-done = f32[768,2000]{0,1:T(8,128)} async-done(((f32[768,2000]{0,1:T(8,128)}), f32[768,2000]{0,1:T(8,128)}) %all-reduce.2.cloned.1.call-update) | async-done | bytes 6144016 | tf_op jit(solution)/shard_map/psum | solution.py:27
  304.1 3.0 convert_element_type.10
  307.1 0.1 dynamic-slice_convert_fusion
  307.2 0.0 copy-done
  307.2 3.5 multiply_reduce_fusion
  310.7 0.1 reshape.19
  310.8 0.1 multiply_reduce_fusion.1
  310.9 1.0 constant_dynamic-slice_fusion
  311.9 0.9 copy.18
  312.8 76.0 %psum.15 = f32[16]{0:T(128)S(1)} all-reduce(f32[16]{0:T(128)S(1)} %multiply_reduce_fusion.1), channel_id=1, replica_groups=mesh['band'=16,'gvec'=16] {'band','gvec'}, use_global_device_ids=true, to_apply=%region_4.5 | all-reduce | flops 16 | bytes 128 | tf_op jit(solution)/shard_map/psum | solution.py:38
  388.8 0.5 negate_multiply_fusion
  (3 shorter events, 0.0 us)
Async XLA Ops:
  7.2 300.0 %copy-start = (bf16[4,125,2000]{2,0,1:T(4,128)(2,1)S(1)}, bf16[4,125,2000]{2,0,1:T(4,128)(2,1)}, u32[]{:S(2)}) copy-start(bf16[4,125,2000]{2,0,1:T(4,128)(2,1)} %param.8) | copy-start | bytes 6000004
  7.2 95.7 %all-gather.3.cloned.1.call-start = ((), (), s32[]{:S(2)}) async-start(), calls=%async_computation.1 | async-start | bytes 16328704 | tf_op jit(solution)/shard_map/all_gather | solution.py:21
  7.9 296.1 %all-reduce.2.cloned.1.call-start = ((), (), s32[]{:S(2)}) async-start(), calls=%async_computation | async-start | bytes 12288000 | tf_op jit(solution)/shard_map/psum | solution.py:27
  174.7 0.7 copy-start.1
  174.7 0.9 copy-start.2
Sparse Core Ops, SparseCore 0:
  9.9 92.9 all-gather.2
  174.9 129.1 all-reduce.1
where the time goes:
time: 397 us; the launch traced here: 396 us
  waiting for transfers between devices  223 us (56%)
  blocking collectives  76 us (19%)
  local copies, waits for them, and re-layouts  55.3 us (14%)
  matrix products  23.1 us (6%)
  between operations  14.7 us (4%)
    psum x1, waiting for transfers between devices, local(): summed = lax.psum(partial_sum, 'gvec')  128 us
    all_gather x1, waiting for transfers between devices, local(): lax.all_gather(eigvecs, 'band', axis=1, tiled=True)  94.1 us
    psum x1, blocking collectives, local(): total = lax.psum(terms, ('band', 'gvec'))  76 us
    unnamed x8, local copies, waits for them, and re-layouts  29 us
    all_gather x1, local copies, waits for them, and re-layouts, local(): lax.all_gather(eigvecs, 'band', axis=1, tiled=True)  24 us
    dot_general x1, matrix products, local(): jnp.dot(flat_rows, lax.all_gather(eigvecs, 'band', axis=1, tiled=True), p...  19.6 us
  transfers between devices with their start and end apart: 2, of which 2 were waited for; matrix products, arithmetic and copies ran while one was open for 0% of the time, Pallas kernels for 0%

commit v1 on v0

v1 whole, which is shorter than its diff:
```python
import math

import jax
import jax.numpy as jnp
from jax import lax
from jax.experimental import pallas as pl
from jax.experimental.pallas import tpu as pltpu
from jax.sharding import PartitionSpec as P

NEIG = 2000
LANES = 128
LIMIT = 32000.0
STEPS = 24
SIDE = 4
HALF = 1872
VMEM = 48 * 1024 * 1024


def project_kernel(layout, cols, pd_ref, *refs):
    pieces, out_ref, rhs = refs[: len(layout)], refs[-2], refs[-1]

    @pl.when(pl.program_id(0) == 0)
    def _():
        for piece, (row, lane) in zip(pieces, layout):
            rhs[row : row + piece.shape[0], lane : lane + LANES] = piece[...]

    total = jnp.dot(pd_ref[...], rhs[...], preferred_element_type=jnp.float32)
    most = jnp.max(jnp.abs(total), axis=1, keepdims=True)
    scale = jnp.ones_like(most)
    power = jnp.zeros(most.shape, jnp.int32)
    for i in range(1, STEPS + 1):
        fits = most * float(2**i) <= LIMIT
        scale = jnp.where(fits, float(2**i), scale)
        power = jnp.where(fits, i, power)
    code = jnp.round(total * scale).astype(jnp.int32).astype(jnp.int16)
    parts, rows = out_ref.shape[:2]
    out_ref[:, :, 0:cols] = code.reshape(parts, rows, cols)
    wide = jnp.broadcast_to(power, (power.shape[0], LANES)).astype(jnp.int16)
    out_ref[:, :, cols : cols + LANES] = wide.reshape(parts, rows, LANES)


def project(flat, pieces, layout, cols, devices):
    nrows, depth = flat.shape
    split = 2
    block = nrows // split
    share = nrows // devices
    return pl.pallas_call(
        lambda *refs: project_kernel(layout, cols, *refs),
        grid=(split,),
        in_specs=[pl.BlockSpec((block, depth), lambda i: (i, 0))]
        + [pl.BlockSpec(p.shape, lambda i: (0, 0)) for p in pieces],
        out_specs=pl.BlockSpec((devices // split, share, cols + LANES), lambda i: (i, 0, 0)),
        out_shape=jax.ShapeDtypeStruct((devices, share, cols + LANES), jnp.int16),
        scratch_shapes=[pltpu.VMEM((depth, cols), jnp.bfloat16)],
        compiler_params=pltpu.CompilerParams(vmem_limit_bytes=VMEM),
        cost_estimate=pl.CostEstimate(
            flops=2 * nrows * depth * cols, bytes_accessed=2 * nrows * depth + 2 * depth * cols, transcendentals=0
        ),
        name="project",
    )(flat, *pieces)


def collect_kernel(code_ref, live_ref, coef_ref, rounded_ref):
    devices, rows, width = code_ref.shape
    cols = width - LANES
    total = jnp.zeros((rows, cols), jnp.float32)
    for d in range(devices):
        power = code_ref[d, :, cols : cols + LANES].astype(jnp.int32)[:, 0:1]
        unit = 1.0 / (jnp.ones_like(power) << power).astype(jnp.float32)
        total += code_ref[d, :, 0:cols].astype(jnp.int32).astype(jnp.float32) * unit
    total = total * live_ref[...]
    for n in range(cols // LANES):
        part = total[:, n * LANES : (n + 1) * LANES]
        coef_ref[n] = part
        rounded_ref[n] = part.astype(jnp.bfloat16)


def collect(code, live_rows):
    devices, rows, width = code.shape
    blocks = (width - LANES) // LANES
    return pl.pallas_call(
        collect_kernel,
        out_shape=(
            jax.ShapeDtypeStruct((blocks, rows, LANES), jnp.float32),
            jax.ShapeDtypeStruct((blocks, rows, LANES), jnp.bfloat16),
        ),
        compiler_params=pltpu.CompilerParams(vmem_limit_bytes=VMEM),
        name="collect",
    )(code, live_rows)


def quad_kernel(share, place_ref, own_ref, w_ref, pick_ref, coef_ref, *refs):
    pieces, out_ref, flat = refs[:SIDE], refs[SIDE], refs[SIDE + 1]
    rows = pieces[0].shape[1]
    blocks = pieces[0].shape[0]
    for k in range(blocks):
        at = place_ref[k]
        out_ref[k, 0:rows, :] = coef_ref[at]
        for d, piece in enumerate(pieces):
            flat[d * rows : (d + 1) * rows, k * share : (k + 1) * share] = piece[at][:, 0:share]
    total = jnp.zeros((SIDE * rows, 1), jnp.float32)
    for p in range(SIDE):
        at = own_ref[p]
        left = jnp.concatenate([piece[at] for piece in pieces], axis=0)[:, 0:share].astype(jnp.float32)
        for node in range(w_ref.shape[1]):
            applied = lax.dot_general(
                flat[...], w_ref[p, node], (((1,), (1,)), ((), ())), preferred_element_type=jnp.float32
            )
            total += jnp.sum(left * applied, axis=1, keepdims=True) * pick_ref[node]
    states = 16
    terms = jnp.sum(total.reshape(SIDE * rows // states, states, 1), axis=0)
    wide = jnp.broadcast_to(terms, (states, LANES))
    for k in range(blocks):
        out_ref[k, rows : rows + states, :] = wide


def quadratic(place, own, gathered, pick, coef, pieces, share):
    blocks, rows, _ = pieces[0].shape
    smem = pl.BlockSpec(memory_space=pltpu.SMEM)
    vmem = pl.BlockSpec(memory_space=pltpu.VMEM)
    return pl.pallas_call(
        lambda *refs: quad_kernel(share, *refs),
        in_specs=[smem, smem] + [vmem] * (3 + SIDE),
        out_specs=vmem,
        out_shape=jax.ShapeDtypeStruct((blocks, rows + 16, LANES), jnp.float32),
        scratch_shapes=[pltpu.VMEM((SIDE * rows, blocks * share), jnp.bfloat16)],
        compiler_params=pltpu.CompilerParams(vmem_limit_bytes=VMEM),
        name="quad",
    )(place, own, gathered, pick, coef, *pieces)


def local(pair_density, eigvecs, subspace, counts, freq_index, band_weight):
    slots, states, depth = pair_density.shape
    nodes, share, neig = subspace.shape
    devices = lax.axis_size("gvec")
    bands = lax.axis_size("band")
    chips = bands // 2
    nrows = slots * states
    rows = nrows // devices
    band, gvec = lax.axis_index("band"), lax.axis_index("gvec")
    zed, core = band >> 1, band & 1
    why, ex = gvec >> 2, gvec & 3

    def shift(value, by):
        return lax.ppermute(value, "band", [(b, (b + 2 * by) % bands) for b in range(bands)])

    def sibling(value):
        return lax.ppermute(value, "band", [(b, b ^ 1) for b in range(bands)])

    def along_y(value, by):
        return lax.ppermute(value, "gvec", [(g, (g + SIDE * by) % devices) for g in range(devices)])

    flat = pair_density.reshape(nrows, depth)
    mine = jnp.pad(eigvecs, ((0, 0), (0, LANES - share)))
    lines = [[g for g in range(devices) if g // SIDE == y] for y in range(SIDE)]
    gathered = lax.all_gather(subspace, "gvec", axis_index_groups=lines)

    live = (jnp.arange(slots, dtype=jnp.int32) < counts[0]).astype(jnp.float32)
    live_rows = jnp.repeat(live, states).reshape(devices, rows, 1)
    weight_rows = jnp.repeat(band_weight * live, states).reshape(devices, rows)
    freq_rows = freq_index.reshape(devices, rows)
    order = [(((why - d) & (SIDE - 1)) * SIDE + ex) for d in range(SIDE)]
    freq_here = jnp.concatenate([lax.dynamic_index_in_dim(freq_rows, p, 0, False) for p in order])
    weight_here = jnp.concatenate([lax.dynamic_index_in_dim(weight_rows, p, 0, False) for p in order])
    pick = jnp.where(
        freq_here[None, :] == jnp.arange(nodes, dtype=jnp.int32)[:, None], weight_here[None, :], jnp.float32(0.0)
    )[:, :, None]
    live_here = lax.dynamic_index_in_dim(live_rows, gvec, 0, False)

    full = [(0, 0)]
    halves = [(0, 0), (HALF, 0)]

    def lay(forms):
        return [(row, n * LANES) for n, form in enumerate(forms) for row, _ in form]

    ids = [2 * zed + core, 2 * zed + 1 - core]
    up = down = mine
    codes = []

    def send(pieces, forms):
        code = project(flat, pieces, lay(forms), len(forms) * LANES, devices)
        codes.append(lax.all_to_all(code, "gvec", 0, 0))

    held = [mine, sibling(mine)]
    forms = [full, full]
    for step in range(1, chips // 2 + 1):
        last = step == chips // 2
        up = shift(up[:HALF] if last else up, 1)
        down = shift(down[HALF:] if last else down, -1)
        send(held, forms)
        up_z, down_z = 2 * ((zed - step) & (chips - 1)), 2 * ((zed + step) & (chips - 1))
        if last:
            held = [up, down, sibling(up), sibling(down)]
            forms = [halves, halves]
            ids += [up_z + core, up_z + 1 - core]
        else:
            held = [up, sibling(up), down, sibling(down)]
            forms = [full] * 4
            ids += [up_z + core, up_z + 1 - core, down_z + core, down_z + 1 - core]
    send(held, forms)

    parts = [collect(code, live_here) for code in codes]
    coef = jnp.concatenate([p[0] for p in parts], axis=0)
    rounded = jnp.concatenate([p[1] for p in parts], axis=0)
    around = [rounded] + [along_y(rounded, d) for d in range(1, SIDE)]
    ids = jnp.stack(ids).astype(jnp.int32)
    span = jnp.arange(bands, dtype=jnp.int32)
    place = jnp.sum(jnp.where(ids[None, :] == span[:, None], span[None, :], 0), axis=1)
    own = lax.dynamic_slice_in_dim(place, why * SIDE, SIDE, 0)
    message = quadratic(place, own, gathered, pick, coef, around, share)
    landed = lax.all_to_all(message, "gvec", 0, 0)
    coef_out = landed[:, 0:rows, 0:share].reshape(slots, states, share)
    terms = jnp.sum(landed[:, rows : rows + states, 0], axis=0)
    spread = lax.all_to_all(jnp.broadcast_to(terms, (bands, states)), "band", 0, 0)
    total = jnp.sum(spread, axis=0)
    scale_factor = math.sqrt(NEIG * bands * slots)
    sigma = -total / jnp.float32(scale_factor)
    return (coef_out, sigma)


def solution(mesh):
    in_specs = (
        P("band", None, "gvec"),
        P("gvec", "band"),
        P(None, "gvec", None),
        P("band"),
        P("band", None),
        P("band"),
    )
    out_specs = (P("band", None, "gvec"), P())
    return jax.shard_map(local, mesh=mesh, in_specs=in_specs, out_specs=out_specs, check_vma=False)
```

time: 397 us -> 237 us (0.60)
  waiting for transfers between devices: 223 us -> 50 us
  starting transfers between devices: 0.08 us -> 64.3 us
  blocking collectives: 76 us -> 14.4 us
  Pallas kernels: 0 us -> 46.4 us
  matrix products: 23.1 us -> 0 us
  local copies, waits for them, and re-layouts: 55.3 us -> 40.9 us
    psum x1 -> x0, waiting for transfers between devices: 128 us -> none  [local(): summed = lax.psum(partial_sum, 'gvec')]
    all_gather x1, waiting for transfers between devices: 94.1 us -> 0.01 us  [local(): gathered = lax.all_gather(subspace, 'gvec', axis_index_groups=lines)]
    psum x1 -> x0, blocking collectives: 76 us -> none  [local(): total = lax.psum(terms, ('band', 'gvec'))]
    pallas_call x0 -> x11, Pallas kernels: none -> 46.4 us  [the longest x5 38 us: project(): pl.pallas_call(lambda *refs: project_kernel(layout, cols, *refs), grid=(s...]
    all_to_all x0 -> x6, starting transfers between devices: none -> 38.7 us  [the longest x5 30.5 us: send(): codes.append(lax.all_to_all(code, 'gvec', 0, 0))]
    ppermute x0 -> x20, waiting for transfers between devices: none -> 26.6 us  [the longest x8 26.6 us: shift(): lax.ppermute(value, 'band', [(b, (b + 2 * by) % bands) for b in range(ban...]
    ppermute x0 -> x20, starting transfers between devices: none -> 25.6 us  [the longest x8 14.6 us: shift(): lax.ppermute(value, 'band', [(b, (b + 2 * by) % bands) for b in range(ban...]
    all_to_all x0 -> x6, waiting for transfers between devices: none -> 23.4 us  [the longest x5 17.1 us: send(): codes.append(lax.all_to_all(code, 'gvec', 0, 0))]
  transfers between devices with their start and end apart: 2 -> 27, of which waited for: 2 -> 7; matrix products, arithmetic and copies ran while one was open for 0% -> 13% of each run, Pallas kernels for 0% -> 17%
where the time goes in v1:
time: 237 us; the launch traced here: 235 us
  starting transfers between devices  64.3 us (27%)
  waiting for transfers between devices  50 us (21%)
  Pallas kernels  46.4 us (20%)
  local copies, waits for them, and re-layouts  40.9 us (17%)
  between operations  15 us (6%)
  blocking collectives  14.4 us (6%)
  other arithmetic  4.36 us (2%)
    pallas_call x5, Pallas kernels, project(): pl.pallas_call(lambda *refs: project_kernel(layout, cols, *refs), grid=(s...  38 us
    all_to_all x5, starting transfers between devices, send(): codes.append(lax.all_to_all(code, 'gvec', 0, 0))  30.5 us
    ppermute x8, waiting for transfers between devices, shift(): lax.ppermute(value, 'band', [(b, (b + 2 * by) % bands) for b in range(ban...  26.6 us
    all_to_all x5, waiting for transfers between devices, send(): codes.append(lax.all_to_all(code, 'gvec', 0, 0))  17.1 us
    unnamed x38, local copies, waits for them, and re-layouts  16.6 us
    ppermute x8, starting transfers between devices, shift(): lax.ppermute(value, 'band', [(b, (b + 2 * by) % bands) for b in range(ban...  14.6 us
    all_to_all x1, blocking collectives, local(): landed = lax.all_to_all(message, 'gvec', 0, 0)  14.4 us
    all_gather x1, local copies, waits for them, and re-layouts, local(): gathered = lax.all_gather(subspace, 'gvec', axis_index_groups=lines)  12.5 us
  transfers between devices with their start and end apart: 27, of which 7 were waited for; matrix products, arithmetic and copies ran while one was open for 13% of the time, Pallas kernels for 17%

profile of v1, /device:TPU:1, one launch (start us, length us, event | category | flops | bytes accessed | tf_op | source)
XLA Modules:
  0.0 235.4 jit_solution(13774803508658364154)
XLA Ops:
  7.2 4.6 %copy.37 = bf16[4,125,2000]{1,2,0:T(8,128)(2,1)} copy(bf16[4,125,2000]{2,0,1:T(4,128)(2,1)} %param.8) | data formatting | bytes 4000000 | tf_op args[2]
  12.1 2.5 %collective-permute-start.1 = (bf16[3750,128]{1,0:T(8,128)(2,1)S(1)}, bf16[3750,128]{1,0:T(8,128)(2,1)}, u32[]{:S(2)}, u32[]{:S(2)}) collective-permute-start(bf16[3750,128]{1,0:T(8,128)(2,1)S(1)} %pad.4.refs_1_), channel_id=1, source_target_pairs={{0,32},{16,48},{32,64},{48,80},{64,96},{80,112},{96,128},{112,144}... | collective-permute-start | bytes 2880008 | tf_op jit(solution)/shard_map/ppermute | solution.py:145
  14.6 4.0 %collective-permute-start.3 = (bf16[3750,128]{1,0:T(8,128)(2,1)S(1)}, bf16[3750,128]{1,0:T(8,128)(2,1)}, u32[]{:S(2)}, u32[]{:S(2)}) collective-permute-start(bf16[3750,128]{1,0:T(8,128)(2,1)S(1)} %pad.4.refs_1_), channel_id=1, source_target_pairs={{0,224},{16,240},{32,0},{48,16},{64,32},{80,48},{96,64},{112,80},{... | collective-permute-start | bytes 2880008 | tf_op jit(solution)/shard_map/ppermute | solution.py:145
  19.6 20.1 %collective-permute-done.1.refs_1_ = bf16[3750,128]{1,0:T(8,128)(2,1)} collective-permute-done((bf16[3750,128]{1,0:T(8,128)(2,1)S(1)}, bf16[3750,128]{1,0:T(8,128)(2,1)}, u32[]{:S(2)}, u32[]{:S(2)}) %collective-permute-start.1) | collective-permute-done | bytes 960032 | tf_op jit(solution)/shard_map/ppermute | solution.py:145
  39.7 2.7 %collective-permute-start.7 = (bf16[3750,128]{1,0:T(8,128)(2,1)}, bf16[3750,128]{1,0:T(8,128)(2,1)}, u32[]{:S(2)}, u32[]{:S(2)}) collective-permute-start(bf16[3750,128]{1,0:T(8,128)(2,1)} %collective-permute-done.3.refs_3_), channel_id=1, source_target_pairs={{0,224},{16,240},{32,0},{48,16},{64,32},{80,48},{96,64},{112,80},{... | collective-permute-start | bytes 2880008 | tf_op jit(solution)/shard_map/ppermute | solution.py:145
  42.4 1.8 collective-permute-start.2
  44.2 6.1 %project.5 = s16[16,48,384]{2,1,0:T(8,128)(2,1)} custom-call(bf16[768,3750]{1,0:T(8,128)(2,1)} %bitcast.42, bf16[3750,128]{1,0:T(8,128)(2,1)S(1)} %pad.4.refs_1_, bf16[3750,128]{1,0:T(8,128)(2,1)S(1)} %collective-permute-done.refs_2_), custom_call_target="tpu_custom_call" | custom-call | flops 1474560000 | bytes 7680000 | tf_op jit(solution)/shard_map/project/pallas_call | solution.py:47
  50.2 6.8 %all-to-all-start = ((s16[16,48,384]{2,1,0:T(8,128)(2,1)}), s16[16,48,384]{2,1,0:T(8,128)(2,1)S(1)}, u32[]{:S(2)}, u32[]{:S(2)}) async-start(s16[16,48,384]{2,1,0:T(8,128)(2,1)} %project.5), calls=%async_computation | async-start | bytes 1179648 | tf_op jit(solution)/shard_map/all_to_all | solution.py:182
  57.0 5.7 %collective-permute-done.5.refs_1_ = bf16[3750,128]{1,0:T(8,128)(2,1)} collective-permute-done((bf16[3750,128]{1,0:T(8,128)(2,1)}, bf16[3750,128]{1,0:T(8,128)(2,1)}, u32[]{:S(2)}, u32[]{:S(2)}) %collective-permute-start.5) | collective-permute-done | bytes 960032 | tf_op jit(solution)/shard_map/ppermute | solution.py:145
  62.7 2.7 %collective-permute-start.11 = (bf16[3750,128]{1,0:T(8,128)(2,1)}, bf16[3750,128]{1,0:T(8,128)(2,1)S(1)}, u32[]{:S(2)}, u32[]{:S(2)}) collective-permute-start(bf16[3750,128]{1,0:T(8,128)(2,1)} %collective-permute-done.7.refs_3_), channel_id=1, source_target_pairs={{0,224},{16,240},{32,0},{48,16},{64,32},{80,48},{96,64},{112,80},{... | collective-permute-start | bytes 2880008 | tf_op jit(solution)/shard_map/ppermute | solution.py:145
  65.4 2.7 %collective-permute-start.6 = (bf16[3750,128]{1,0:T(8,128)(2,1)}, bf16[3750,128]{1,0:T(8,128)(2,1)}, u32[]{:S(2)}, u32[]{:S(2)}) collective-permute-start(bf16[3750,128]{1,0:T(8,128)(2,1)} %collective-permute-done.5.refs_1_), channel_id=1, source_target_pairs={{0,16},{16,0},{32,48},{48,32},{64,80},{80,64},{96,112},{112,96},{1... | collective-permute-start | bytes 2880008 | tf_op jit(solution)/shard_map/ppermute | solution.py:148
  68.1 9.1 %project.6 = s16[16,48,640]{2,1,0:T(8,128)(2,1)} custom-call(bf16[768,3750]{1,0:T(8,128)(2,1)} %bitcast.43, bf16[3750,128]{1,0:T(8,128)(2,1)} %collective-permute-done.1.refs_1_, bf16[3750,128]{1,0:T(8,128)(2,1)} %collective-permute-done.2.refs_2_, bf16[3750,128]{1,0:T(8,128)(2,1)} %collective-permute-done.3.refs_3_, ...), custom_call_target="tpu_custom_call" | custom-call | flops 2949120000 | bytes 9600000 | tf_op jit(solution)/shard_map/project/pallas_call | solution.py:47
  77.3 6.8 %all-to-all-start.1 = ((s16[16,48,640]{2,1,0:T(8,128)(2,1)}), s16[16,48,640]{2,1,0:T(8,128)(2,1)S(1)}, u32[]{:S(2)}, u32[]{:S(2)}) async-start(s16[16,48,640]{2,1,0:T(8,128)(2,1)} %project.6), calls=%async_computation.1 | async-start | bytes 1966080 | tf_op jit(solution)/shard_map/all_to_all | solution.py:182
  84.9 1.9 slice.16
  88.5 2.7 %collective-permute-start.14 = (bf16[1878,128]{1,0:T(8,128)(2,1)}, bf16[1878,128]{1,0:T(8,128)(2,1)S(1)}, u32[]{:S(2)}, u32[]{:S(2)}) collective-permute-start(bf16[1878,128]{1,0:T(8,128)(2,1)} %slice.17), channel_id=1, source_target_pairs={{0,224},{16,240},{32,0},{48,16},{64,32},{80,48},{96,64},{112,80},{... | collective-permute-start | bytes 1442312 | tf_op jit(solution)/shard_map/ppermute | solution.py:145
  91.2 9.2 %project.7 = s16[16,48,640]{2,1,0:T(8,128)(2,1)} custom-call(bf16[768,3750]{1,0:T(8,128)(2,1)} %bitcast.44, bf16[3750,128]{1,0:T(8,128)(2,1)} %collective-permute-done.5.refs_1_, bf16[3750,128]{1,0:T(8,128)(2,1)} %collective-permute-done.6.refs_2_, bf16[3750,128]{1,0:T(8,128)(2,1)} %collective-permute-done.7.refs_3_, ...), custom_call_target="tpu_custom_call" | custom-call | flops 2949120000 | bytes 9600000 | tf_op jit(solution)/shard_map/project/pallas_call | solution.py:47
  100.4 10.7 %all-to-all-done.1.code_ref = s16[16,48,640]{2,1,0:T(8,128)(2,1)S(1)} async-done(((s16[16,48,640]{2,1,0:T(8,128)(2,1)}), s16[16,48,640]{2,1,0:T(8,128)(2,1)S(1)}, u32[]{:S(2)}, u32[]{:S(2)}) %all-to-all-start.1) | async-done | bytes 983072 | tf_op jit(solution)/shard_map/all_to_all | solution.py:182
  111.1 3.6 %all-to-all-start.2 = ((s16[16,48,640]{2,1,0:T(8,128)(2,1)}), s16[16,48,640]{2,1,0:T(8,128)(2,1)S(1)}, u32[]{:S(2)}, u32[]{:S(2)}) async-start(s16[16,48,640]{2,1,0:T(8,128)(2,1)} %project.7), calls=%async_computation.2 | async-start | bytes 1966080 | tf_op jit(solution)/shard_map/all_to_all | solution.py:182
  115.4 1.7 collective-permute-start.10
  120.8 1.4 fusion.6
  122.7 5.6 %project.9 = s16[16,48,384]{2,1,0:T(8,128)(2,1)S(1)} custom-call(bf16[768,3750]{1,0:T(8,128)(2,1)} %bitcast.45, bf16[1872,128]{1,0:T(8,128)(2,1)} %collective-permute-done.13.refs_1_, bf16[1878,128]{1,0:T(8,128)(2,1)S(1)} %collective-permute-done.14.refs_2_, bf16[1872,128]{1,0:T(8,128)(2,1)} %collective-permute-done.15.refs_3_, ...), custom_call_target="tpu_custom_call" | custom-call | flops 1474560000 | bytes 7680000 | tf_op jit(solution)/shard_map/project/pallas_call | solution.py:47
  129.4 6.6 %all-to-all-start.4 = ((s16[16,48,384]{2,1,0:T(8,128)(2,1)}), s16[16,48,384]{2,1,0:T(8,128)(2,1)S(1)}, u32[]{:S(2)}, u32[]{:S(2)}) async-start(s16[16,48,384]{2,1,0:T(8,128)(2,1)} %copy-done.2), calls=%async_computation.4 | async-start | bytes 1179648 | tf_op jit(solution)/shard_map/all_to_all | solution.py:182
  139.6 8.1 %project.8 = s16[16,48,640]{2,1,0:T(8,128)(2,1)S(1)} custom-call(bf16[768,3750]{1,0:T(8,128)(2,1)} %bitcast.46, bf16[3750,128]{1,0:T(8,128)(2,1)} %collective-permute-done.9.refs_1_, bf16[3750,128]{1,0:T(8,128)(2,1)} %collective-permute-done.10.refs_2_, bf16[3750,128]{1,0:T(8,128)(2,1)S(1)} %copy-done.10, bf16[3750,128]{1,0:T(8,128)(2,1)} %collective-permute-done.12.refs_4_), custom_call_target="tpu_custom_call" | custom-call | flops 2949120000 | bytes 9600000 | tf_op jit(solution)/shard_map/project/pallas_call | solution.py:47
  149.5 6.6 %all-to-all-start.3 = ((s16[16,48,640]{2,1,0:T(8,128)(2,1)}), s16[16,48,640]{2,1,0:T(8,128)(2,1)S(1)}, u32[]{:S(2)}, u32[]{:S(2)}) async-start(s16[16,48,640]{2,1,0:T(8,128)(2,1)} %copy-done.4), calls=%async_computation.3 | async-start | bytes 1966080 | tf_op jit(solution)/shard_map/all_to_all | solution.py:182
  158.1 1.5 fusion.refs_3_
  165.0 6.1 %all-to-all-done.3.code_ref = s16[16,48,640]{2,1,0:T(8,128)(2,1)S(1)} async-done(((s16[16,48,640]{2,1,0:T(8,128)(2,1)}), s16[16,48,640]{2,1,0:T(8,128)(2,1)S(1)}, u32[]{:S(2)}, u32[]{:S(2)}) %all-to-all-start.3) | async-done | bytes 983072 | tf_op jit(solution)/shard_map/all_to_all | solution.py:182
  173.4 2.0 collective-permute-start.18
  177.8 12.5 %copy.38 = bf16[16,125,2000]{2,1,0:T(8,128)(2,1)} copy(bf16[16,125,2000]{1,2,0:T(8,128)(2,1)} %all-gather.3.cloned.1.call-done) | data formatting | bytes 16000000 | tf_op jit(solution)/shard_map/all_gather | solution.py:156
  190.4 7.2 %quad.1 = f32[16,64,128]{2,1,0:T(8,128)S(1)} custom-call(s32[16]{0:T(128)S(1)} %select_reduce_fusion.refs_0_, s32[4]{0:T(128)S(1)} %dynamic_slice.31.refs_1_, bf16[4,4,125,2000]{3,2,1,0:T(8,128)(2,1)} %bitcast.41, f32[4,192,1]{2,1,0:T(8,128)S(1)} %copy-done.3, f32[16,48,128]{2,1,0:T(8,128)} %constant_dynamic-update-slice_fusion.refs_4_, ...), custom_call_target="tpu_custom_call" | custom-call | tf_op jit(solution)/shard_map/quad/pallas_call | solution.py:121
  197.6 14.4 %all_to_all.36 = f32[16,64,128]{2,1,0:T(8,128)S(1)} all-to-all(f32[16,64,128]{2,1,0:T(8,128)S(1)} %quad.1), channel_id=1, replica_groups=mesh['band'=16,'gvec'=16] {'gvec'}, dimensions={0} | all-to-all | bytes 1048576 | tf_op jit(solution)/shard_map/all_to_all | solution.py:211
  212.8 8.2 %all-to-all-start.6 = ((f32[16,1,16]{2,1,0:T(1,128)}), f32[16,1,16]{2,1,0:T(1,128)S(1)}, u32[]{:S(2)}, u32[]{:S(2)}) async-start(f32[16,1,16]{2,1,0:T(1,128)} %broadcast_in_dim.55), calls=%async_computation.6 | async-start | bytes 16384 | tf_op jit(solution)/shard_map/all_to_all | solution.py:214
  221.8 6.3 %all-to-all-done.6 = f32[16,1,16]{2,1,0:T(1,128)S(1)} async-done(((f32[16,1,16]{2,1,0:T(1,128)}), f32[16,1,16]{2,1,0:T(1,128)S(1)}, u32[]{:S(2)}, u32[]{:S(2)}) %all-to-all-start.6) | async-done | bytes 1056 | tf_op jit(solution)/shard_map/all_to_all | solution.py:214
  (102 shorter events, 28.4 us)
Async XLA Ops:
  7.2 4.7 %copy-start.11 = (bf16[3750,125]{1,0:T(8,128)(2,1)S(1)}, bf16[3750,125]{1,0:T(8,128)(2,1)}, u32[]{:S(2)}) copy-start(bf16[3750,125]{1,0:T(8,128)(2,1)} %param.7) | copy-start | bytes 2812504
  7.2 170.7 %all-gather.3.cloned.1.call-start = ((), (), s32[]{:S(2)}) async-start(), calls=%async_computation.7 | async-start | bytes 10240000 | tf_op jit(solution)/shard_map/all_gather | solution.py:156
  12.1 27.6 %collective-permute-start.1 = (bf16[3750,128]{1,0:T(8,128)(2,1)S(1)}, bf16[3750,128]{1,0:T(8,128)(2,1)}, u32[]{:S(2)}, u32[]{:S(2)}) collective-permute-start(bf16[3750,128]{1,0:T(8,128)(2,1)S(1)} %pad.4.refs_1_), channel_id=1, source_target_pairs={{0,32},{16,48},{32,64},{48,80},{64,96},{80,112},{96,128},{112,144}... | collective-permute-start | bytes 2880008 | tf_op jit(solution)/shard_map/ppermute | solution.py:145
  14.6 25.0 %collective-permute-start.3 = (bf16[3750,128]{1,0:T(8,128)(2,1)S(1)}, bf16[3750,128]{1,0:T(8,128)(2,1)}, u32[]{:S(2)}, u32[]{:S(2)}) collective-permute-start(bf16[3750,128]{1,0:T(8,128)(2,1)S(1)} %pad.4.refs_1_), channel_id=1, source_target_pairs={{0,224},{16,240},{32,0},{48,16},{64,32},{80,48},{96,64},{112,80},{... | collective-permute-start | bytes 2880008 | tf_op jit(solution)/shard_map/ppermute | solution.py:145
  18.7 25.5 %collective-permute-start = (bf16[3750,128]{1,0:T(8,128)(2,1)S(1)}, bf16[3750,128]{1,0:T(8,128)(2,1)S(1)}, u32[]{:S(2)}, u32[]{:S(2)}) collective-permute-start(bf16[3750,128]{1,0:T(8,128)(2,1)S(1)} %pad.4.refs_1_), channel_id=1, source_target_pairs={{0,16},{16,0},{32,48},{48,32},{64,80},{80,64},{96,112},{112,96},{1... | collective-permute-start | bytes 2880008 | tf_op jit(solution)/shard_map/ppermute | solution.py:148
  39.7 23.1 %collective-permute-start.5 = (bf16[3750,128]{1,0:T(8,128)(2,1)}, bf16[3750,128]{1,0:T(8,128)(2,1)}, u32[]{:S(2)}, u32[]{:S(2)}) collective-permute-start(bf16[3750,128]{1,0:T(8,128)(2,1)} %collective-permute-done.1.refs_1_), channel_id=1, source_target_pairs={{0,32},{16,48},{32,64},{48,80},{64,96},{80,112},{96,128},{112,144}... | collective-permute-start | bytes 2880008 | tf_op jit(solution)/shard_map/ppermute | solution.py:145
  39.7 23.1 %collective-permute-start.7 = (bf16[3750,128]{1,0:T(8,128)(2,1)}, bf16[3750,128]{1,0:T(8,128)(2,1)}, u32[]{:S(2)}, u32[]{:S(2)}) collective-permute-start(bf16[3750,128]{1,0:T(8,128)(2,1)} %collective-permute-done.3.refs_3_), channel_id=1, source_target_pairs={{0,224},{16,240},{32,0},{48,16},{64,32},{80,48},{96,64},{112,80},{... | collective-permute-start | bytes 2880008 | tf_op jit(solution)/shard_map/ppermute | solution.py:145
  42.4 25.8 %collective-permute-start.2 = (bf16[3750,128]{1,0:T(8,128)(2,1)}, bf16[3750,128]{1,0:T(8,128)(2,1)}, u32[]{:S(2)}, u32[]{:S(2)}) collective-permute-start(bf16[3750,128]{1,0:T(8,128)(2,1)} %collective-permute-done.1.refs_1_), channel_id=1, source_target_pairs={{0,16},{16,0},{32,48},{48,32},{64,80},{80,64},{96,112},{112,96},{1... | collective-permute-start | bytes 2880008 | tf_op jit(solution)/shard_map/ppermute | solution.py:148
  44.1 24.0 %collective-permute-start.4 = (bf16[3750,128]{1,0:T(8,128)(2,1)}, bf16[3750,128]{1,0:T(8,128)(2,1)}, u32[]{:S(2)}, u32[]{:S(2)}) collective-permute-start(bf16[3750,128]{1,0:T(8,128)(2,1)} %collective-permute-done.3.refs_3_), channel_id=1, source_target_pairs={{0,16},{16,0},{32,48},{48,32},{64,80},{80,64},{96,112},{112,96},{1... | collective-permute-start | bytes 2880008 | tf_op jit(solution)/shard_map/ppermute | solution.py:148
  50.2 27.1 %all-to-all-start = ((s16[16,48,384]{2,1,0:T(8,128)(2,1)}), s16[16,48,384]{2,1,0:T(8,128)(2,1)S(1)}, u32[]{:S(2)}, u32[]{:S(2)}) async-start(s16[16,48,384]{2,1,0:T(8,128)(2,1)} %project.5), calls=%async_computation | async-start | bytes 1179648 | tf_op jit(solution)/shard_map/all_to_all | solution.py:182
  62.7 22.1 %collective-permute-start.9 = (bf16[3750,128]{1,0:T(8,128)(2,1)}, bf16[3750,128]{1,0:T(8,128)(2,1)}, u32[]{:S(2)}, u32[]{:S(2)}) collective-permute-start(bf16[3750,128]{1,0:T(8,128)(2,1)} %collective-permute-done.5.refs_1_), channel_id=1, source_target_pairs={{0,32},{16,48},{32,64},{48,80},{64,96},{80,112},{96,128},{112,144}... | collective-permute-start | bytes 2880008 | tf_op jit(solution)/shard_map/ppermute | solution.py:145
  62.7 24.0 %collective-permute-start.11 = (bf16[3750,128]{1,0:T(8,128)(2,1)}, bf16[3750,128]{1,0:T(8,128)(2,1)S(1)}, u32[]{:S(2)}, u32[]{:S(2)}) collective-permute-start(bf16[3750,128]{1,0:T(8,128)(2,1)} %collective-permute-done.7.refs_3_), channel_id=1, source_target_pairs={{0,224},{16,240},{32,0},{48,16},{64,32},{80,48},{96,64},{112,80},{... | collective-permute-start | bytes 2880008 | tf_op jit(solution)/shard_map/ppermute | solution.py:145
  65.4 25.8 %collective-permute-start.6 = (bf16[3750,128]{1,0:T(8,128)(2,1)}, bf16[3750,128]{1,0:T(8,128)(2,1)}, u32[]{:S(2)}, u32[]{:S(2)}) collective-permute-start(bf16[3750,128]{1,0:T(8,128)(2,1)} %collective-permute-done.5.refs_1_), channel_id=1, source_target_pairs={{0,16},{16,0},{32,48},{48,32},{64,80},{80,64},{96,112},{112,96},{1... | collective-permute-start | bytes 2880008 | tf_op jit(solution)/shard_map/ppermute | solution.py:148
  68.1 23.1 %collective-permute-start.8 = (bf16[3750,128]{1,0:T(8,128)(2,1)}, bf16[3750,128]{1,0:T(8,128)(2,1)}, u32[]{:S(2)}, u32[]{:S(2)}) collective-permute-start(bf16[3750,128]{1,0:T(8,128)(2,1)} %collective-permute-done.7.refs_3_), channel_id=1, source_target_pairs={{0,16},{16,0},{32,48},{48,32},{64,80},{80,64},{96,112},{112,96},{1... | collective-permute-start | bytes 2880008 | tf_op jit(solution)/shard_map/ppermute | solution.py:148
  77.3 33.8 %all-to-all-start.1 = ((s16[16,48,640]{2,1,0:T(8,128)(2,1)}), s16[16,48,640]{2,1,0:T(8,128)(2,1)S(1)}, u32[]{:S(2)}, u32[]{:S(2)}) async-start(s16[16,48,640]{2,1,0:T(8,128)(2,1)} %project.6), calls=%async_computation.1 | async-start | bytes 1966080 | tf_op jit(solution)/shard_map/all_to_all | solution.py:182
  86.8 30.5 %collective-permute-start.13 = (bf16[1872,128]{1,0:T(8,128)(2,1)}, bf16[1872,128]{1,0:T(8,128)(2,1)}, u32[]{:S(2)}, u32[]{:S(2)}) collective-permute-start(bf16[1872,128]{1,0:T(8,128)(2,1)} %slice.16), channel_id=1, source_target_pairs={{0,32},{16,48},{32,64},{48,80},{64,96},{80,112},{96,128},{112,144}... | collective-permute-start | bytes 1437704 | tf_op jit(solution)/shard_map/ppermute | solution.py:145
  88.5 29.2 %copy-start.13 = (f32[48]{0:T(128)S(1)}, f32[48]{0:T(128)}, u32[]{:S(2)}) copy-start(f32[48]{0:T(128)} %param.11) | copy-start | bytes 580
  88.5 29.1 %collective-permute-start.14 = (bf16[1878,128]{1,0:T(8,128)(2,1)}, bf16[1878,128]{1,0:T(8,128)(2,1)S(1)}, u32[]{:S(2)}, u32[]{:S(2)}) collective-permute-start(bf16[1878,128]{1,0:T(8,128)(2,1)} %slice.17), channel_id=1, source_target_pairs={{0,224},{16,240},{32,0},{48,16},{64,32},{80,48},{96,64},{112,80},{... | collective-permute-start | bytes 1442312 | tf_op jit(solution)/shard_map/ppermute | solution.py:145
  111.1 18.2 %all-to-all-start.2 = ((s16[16,48,640]{2,1,0:T(8,128)(2,1)}), s16[16,48,640]{2,1,0:T(8,128)(2,1)S(1)}, u32[]{:S(2)}, u32[]{:S(2)}) async-start(s16[16,48,640]{2,1,0:T(8,128)(2,1)} %project.7), calls=%async_computation.2 | async-start | bytes 1966080 | tf_op jit(solution)/shard_map/all_to_all | solution.py:182
  115.4 23.0 %collective-permute-start.10 = (bf16[3750,128]{1,0:T(8,128)(2,1)}, bf16[3750,128]{1,0:T(8,128)(2,1)}, u32[]{:S(2)}, u32[]{:S(2)}) collective-permute-start(bf16[3750,128]{1,0:T(8,128)(2,1)} %collective-permute-done.9.refs_1_), channel_id=1, source_target_pairs={{0,16},{16,0},{32,48},{48,32},{64,80},{80,64},{96,112},{112,96},{1... | collective-permute-start | bytes 2880008 | tf_op jit(solution)/shard_map/ppermute | solution.py:148
  117.1 21.3 %collective-permute-start.12 = (bf16[3750,128]{1,0:T(8,128)(2,1)}, bf16[3750,128]{1,0:T(8,128)(2,1)}, u32[]{:S(2)}, u32[]{:S(2)}) collective-permute-start(bf16[3750,128]{1,0:T(8,128)(2,1)} %copy-done.9), channel_id=1, source_target_pairs={{0,16},{16,0},{32,48},{48,32},{64,80},{80,64},{96,112},{112,96},{1... | collective-permute-start | bytes 2880008 | tf_op jit(solution)/shard_map/ppermute | solution.py:148
  117.2 5.4 %collective-permute-start.15 = (bf16[1872,128]{1,0:T(8,128)(2,1)}, bf16[1872,128]{1,0:T(8,128)(2,1)}, u32[]{:S(2)}, u32[]{:S(2)}) collective-permute-start(bf16[1872,128]{1,0:T(8,128)(2,1)} %collective-permute-done.13.refs_1_), channel_id=1, source_target_pairs={{0,16},{16,0},{32,48},{48,32},{64,80},{80,64},{96,112},{112,96},{1... | collective-permute-start | bytes 1437704 | tf_op jit(solution)/shard_map/ppermute | solution.py:148
  117.7 5.0 %collective-permute-start.16 = (bf16[1878,128]{1,0:T(8,128)(2,1)S(1)}, bf16[1878,128]{1,0:T(8,128)(2,1)S(1)}, u32[]{:S(2)}, u32[]{:S(2)}) collective-permute-start(bf16[1878,128]{1,0:T(8,128)(2,1)S(1)} %collective-permute-done.14.refs_2_), channel_id=1, source_target_pairs={{0,16},{16,0},{32,48},{48,32},{64,80},{80,64},{96,112},{112,96},{1... | collective-permute-start | bytes 1442312 | tf_op jit(solution)/shard_map/ppermute | solution.py:148
  122.7 13.3 %copy-start.12 = (f32[48]{0:T(128)S(1)}, f32[48]{0:T(128)}, u32[]{:S(2)}) copy-start(f32[48]{0:T(128)} %get-tuple-element.27) | copy-start | bytes 580
  129.4 19.3 %all-to-all-start.4 = ((s16[16,48,384]{2,1,0:T(8,128)(2,1)}), s16[16,48,384]{2,1,0:T(8,128)(2,1)S(1)}, u32[]{:S(2)}, u32[]{:S(2)}) async-start(s16[16,48,384]{2,1,0:T(8,128)(2,1)} %copy-done.2), calls=%async_computation.4 | async-start | bytes 1179648 | tf_op jit(solution)/shard_map/all_to_all | solution.py:182
  149.5 21.6 %all-to-all-start.3 = ((s16[16,48,640]{2,1,0:T(8,128)(2,1)}), s16[16,48,640]{2,1,0:T(8,128)(2,1)S(1)}, u32[]{:S(2)}, u32[]{:S(2)}) async-start(s16[16,48,640]{2,1,0:T(8,128)(2,1)} %copy-done.4), calls=%async_computation.3 | async-start | bytes 1966080 | tf_op jit(solution)/shard_map/all_to_all | solution.py:182
  173.4 17.0 %collective-permute-start.17 = (bf16[16,48,128]{2,1,0:T(8,128)(2,1)}, bf16[16,48,128]{2,1,0:T(8,128)(2,1)S(1)}, u32[]{:S(2)}, u32[]{:S(2)}) collective-permute-start(bf16[16,48,128]{2,1,0:T(8,128)(2,1)} %constant_dynamic-update-slice_fusion.5.refs_5_), channel_id=1, source_target_pairs={{0,4},{1,5},{2,6},{3,7},{4,8},{5,9},{6,10},{7,11},{8,12},{9,13},{1... | collective-permute-start | bytes 589832 | tf_op jit(solution)/shard_map/ppermute | solution.py:151
  173.4 17.0 %collective-permute-start.18 = (bf16[16,48,128]{2,1,0:T(8,128)(2,1)}, bf16[16,48,128]{2,1,0:T(8,128)(2,1)S(1)}, u32[]{:S(2)}, u32[]{:S(2)}) collective-permute-start(bf16[16,48,128]{2,1,0:T(8,128)(2,1)} %constant_dynamic-update-slice_fusion.5.refs_5_), channel_id=1, source_target_pairs={{0,8},{1,9},{2,10},{3,11},{4,12},{5,13},{6,14},{7,15},{8,0},{9,1},... | collective-permute-start | bytes 589832 | tf_op jit(solution)/shard_map/ppermute | solution.py:151
  175.4 15.0 %collective-permute-start.19 = (bf16[16,48,128]{2,1,0:T(8,128)(2,1)}, bf16[16,48,128]{2,1,0:T(8,128)(2,1)S(1)}, u32[]{:S(2)}, u32[]{:S(2)}) collective-permute-start(bf16[16,48,128]{2,1,0:T(8,128)(2,1)} %constant_dynamic-update-slice_fusion.5.refs_5_), channel_id=1, source_target_pairs={{0,12},{1,13},{2,14},{3,15},{4,0},{5,1},{6,2},{7,3},{8,4},{9,5},{1... | collective-permute-start | bytes 589832 | tf_op jit(solution)/shard_map/ppermute | solution.py:151
  177.8 12.5 %copy-start.3 = (f32[4,192,1]{2,1,0:T(8,128)S(1)}, f32[4,192,1]{2,1,0:T(8,128)}, u32[]{:S(2)}) copy-start(f32[4,192,1]{2,1,0:T(8,128)} %fusion.refs_3_) | copy-start | bytes 9220
  177.8 12.5 %copy-start.8 = (bf16[16,48,128]{2,1,0:T(8,128)(2,1)S(1)}, bf16[16,48,128]{2,1,0:T(8,128)(2,1)}, u32[]{:S(2)}) copy-start(bf16[16,48,128]{2,1,0:T(8,128)(2,1)} %constant_dynamic-update-slice_fusion.5.refs_5_) | copy-start | bytes 589828
  212.8 15.2 %all-to-all-start.6 = ((f32[16,1,16]{2,1,0:T(1,128)}), f32[16,1,16]{2,1,0:T(1,128)S(1)}, u32[]{:S(2)}, u32[]{:S(2)}) async-start(f32[16,1,16]{2,1,0:T(1,128)} %broadcast_in_dim.55), calls=%async_computation.6 | async-start | bytes 16384 | tf_op jit(solution)/shard_map/all_to_all | solution.py:214
  (9 other events, 8.0 us)
Sparse Core Ops, SparseCore 0:
  12.0 104.6 all-gather.2
